TPU v7x, 32 devices: a whole 2x2x4 slice. The times are simulated.
32 devices in a mesh: dp: 4 (over z), expert: 4 (over y, x), tensor: 2 (over core).
Axes of the slice: x: 2, y: 2, z: 4, core: 2. Of those that a mesh axis runs over, the one named last changes fastest.
Arguments:
- hidden_in: bfloat16 [4096, 2048], P(('dp', 'expert')), may hold values from -6 to 6
- query: bfloat16 [4096, 2048], P(('dp', 'expert'), 'tensor'), may hold values from -26 to 26
- keys: bfloat16 [4096, 2048], P(('dp', 'expert'), 'tensor'), may hold values from -26 to 26
- values: bfloat16 [4096, 2048], P(('dp', 'expert'), 'tensor'), may hold values from -6 to 6
- out_proj: bfloat16 [2048, 2048], P('tensor'), may hold values from -0.125 to 0.125
- norm_gain: bfloat16 [2048], replicated, may hold values from 0.25 to 1.75
- routes: int32 [4096, 2], P(('dp', 'expert')), may hold values from 0 to 3, all different within a row; in each aligned block of 256 rows (0 to 255, 256 to 511, ...) at most 144 rows name the same one
- gates: float32 [4096, 2], P(('dp', 'expert')), may hold values from 0.2 to 1
- w_gate: bfloat16 [4, 2048, 5504], P('expert', 'dp', 'tensor'), may hold values from -0.125 to 0.125
- w_up: bfloat16 [4, 2048, 5504], P('expert', 'dp', 'tensor'), may hold values from -0.125 to 0.125
- w_down_t: bfloat16 [4, 2048, 5504], P('expert', 'dp', 'tensor'), may hold values from -0.078125 to 0.078125
Outputs:
- layer_out: bfloat16 [4096, 2048], P(('dp', 'expert'), 'tensor')
Inputs may be any that keep to these rules, and one draw needn't show every extreme that they name: `routes`: each row names 2 different experts; in the 256 rows of one block of consecutive tokens no expert is named more than 144 times, a bound that some block reaches.
All inputs are finite; a program needn't handle non-finite values.
Results may differ from a plain program's by a relative error of at most 0.0095.
Values may be sent and summed in bfloat16 or wider, within the bound.
A program may use at most 128 MiB of HBM per device.

v0:
```python
import jax
import jax.numpy as jnp
from jax import lax
from jax.sharding import PartitionSpec as P

HDIM = 128
EPSILON = 1e-05
NEGATIVE = -1e30


def slot_table(block_routes, experts, capacity):
    flat_routes = block_routes.reshape(-1)
    pairs = flat_routes.shape[0]
    onehot = flat_routes[:, None] == jnp.arange(experts, dtype=jnp.int32)[None, :]
    order = jnp.arange(pairs, dtype=jnp.int32)
    earlier = (order[:, None] > order[None, :]).astype(jnp.bfloat16)
    rank_table = jnp.dot(earlier, onehot.astype(jnp.bfloat16), preferred_element_type=jnp.float32)
    slot_index = jnp.sum(jnp.where(onehot, rank_table, 0.0), axis=1).astype(jnp.int32)
    return flat_routes * capacity + slot_index


def attention(query, both, score_scale):
    tok_rows, head_cols = query.shape
    head_count = head_cols // HDIM
    query_pos = lax.axis_index("expert") * tok_rows + jnp.arange(tok_rows, dtype=jnp.int32)
    key_rows, value_rows = (both[:, :head_cols], both[:, head_cols:])
    count_rows = key_rows.shape[0]
    key_pos = jnp.arange(count_rows, dtype=jnp.int32)
    queries = query.reshape(tok_rows, head_count, HDIM)
    key_part = key_rows.reshape(count_rows, head_count, HDIM)
    value_part = value_rows.reshape(count_rows, head_count, HDIM)
    scores = (
        jnp.einsum("qhd,khd->hqk", queries, key_part, preferred_element_type=jnp.float32)
        * score_scale
    )
    causal = (query_pos[:, None] >= key_pos[None, :])[None]
    scores = jnp.where(causal, scores, NEGATIVE)
    new_max = jnp.max(scores, axis=-1)
    weights_now = jnp.where(causal, jnp.exp(scores - new_max[..., None]), 0.0)
    totals = jnp.sum(weights_now, axis=-1)
    weighted = jnp.einsum("hqk,khd->hqd", weights_now, value_part.astype(jnp.float32))
    context = weighted / totals[..., None]
    return jnp.transpose(context, (1, 0, 2)).reshape(tok_rows, head_cols).astype(jnp.bfloat16)


def local(
    hidden_in, query, keys, values, out_proj, norm_gain, routes, gates, w_gate, w_up, w_down_t
):
    tok_rows, feature_width = hidden_in.shape
    top = routes.shape[1]
    experts = lax.axis_size("expert")
    copies = lax.axis_size("dp")
    capacity = 9 * tok_rows // (4 * experts)
    slots = experts * capacity
    tensor_count = lax.axis_size("tensor")
    slice_width = feature_width // tensor_count
    tensor_index = lax.axis_index("tensor")
    shard_rows, hidden_width = w_gate.shape[1:]
    exchange = 2 * tok_rows * feature_width < 3 * shard_rows * hidden_width and copies <= 4
    if hidden_width % copies:
        exchange = False

    def spread(w):
        if not exchange:
            return lax.all_gather(w[0], "dp", axis=0, tiled=True)
        share = hidden_width // copies
        me = lax.axis_index("dp")
        turned = jnp.transpose(w[0]).reshape(copies, share, shard_rows)
        blocks = []
        for step in range(copies):
            block = lax.dynamic_index_in_dim(turned, (me + step) % copies, 0, keepdims=False)
            if step:
                block = lax.ppermute(block, "dp", [(i, (i + step) % copies) for i in range(copies)])
            blocks.append(block)
        stacked = jnp.stack(blocks)
        ordered = [
            lax.dynamic_index_in_dim(stacked, (me - i + copies) % copies, 0, keepdims=False)
            for i in range(copies)
        ]
        return jnp.transpose(jnp.concatenate(ordered, axis=1))

    choice = jnp.concatenate([routes.astype(jnp.float32), gates], axis=1)
    both = lax.all_gather(jnp.concatenate([keys, values], axis=1), "expert", axis=0, tiled=True)
    if exchange:
        choice = lax.all_gather(choice, "dp", axis=0)
        choice, w_gate, w_up, w_down_t = lax.optimization_barrier((choice, w_gate, w_up, w_down_t))
    else:
        choice = choice[None]
    gate_full, up_full, down_full = (spread(w_gate), spread(w_up), spread(w_down_t))
    if exchange:
        both, gate_full = lax.optimization_barrier((both, gate_full))
    context = attention(query, both, 1.0 / HDIM**0.5)
    attended = lax.psum(
        jnp.dot(context, out_proj, preferred_element_type=jnp.float32).astype(jnp.bfloat16),
        "tensor",
    )
    if exchange:
        attended, up_full = lax.optimization_barrier((attended, up_full))
    attended = attended.astype(jnp.float32)
    residual = hidden_in.astype(jnp.float32) + attended
    mean_square = jnp.mean(residual * residual, axis=-1, keepdims=True)
    normed = (residual * lax.rsqrt(mean_square + EPSILON) * norm_gain.astype(jnp.float32)).astype(
        jnp.bfloat16
    )
    own_cols = lax.dynamic_slice_in_dim(normed, tensor_index * slice_width, slice_width, 1)
    own_slice = lax.dynamic_slice_in_dim(residual, tensor_index * slice_width, slice_width, 1)
    blocks = lax.all_gather(own_cols, "dp", axis=0) if exchange else own_cols[None]
    count = blocks.shape[0]
    sends, mixers = ([], [])
    slot_numbers = jnp.arange(slots, dtype=jnp.int32)[:, None]
    for i in range(count):
        picked = choice[i, :, :top].astype(jnp.int32)
        targets = slot_table(picked, experts, capacity).reshape(tok_rows, top)
        place = jnp.zeros((slots, tok_rows), jnp.float32)
        mixing = jnp.zeros((slots, tok_rows), jnp.float32)
        for k in range(top):
            chosen = slot_numbers == targets[:, k][None, :]
            place = jnp.where(chosen, 1.0, place)
            mixing = jnp.where(chosen, choice[i, :, top + k][None, :], mixing)
        sent = jnp.dot(
            place.astype(jnp.bfloat16), blocks[i], preferred_element_type=jnp.float32
        ).astype(jnp.bfloat16)
        sends.append(sent.reshape(experts, capacity, slice_width))
        mixers.append(mixing)
    arrived = lax.all_to_all(
        jnp.concatenate(sends, axis=1), "expert", split_axis=0, concat_axis=0, tiled=True
    ).reshape(count * slots, slice_width)
    if exchange:
        arrived, down_full = lax.optimization_barrier((arrived, down_full))
    halves = lax.all_gather(arrived, "tensor", axis=0)
    slot_rows = jnp.concatenate([halves[i] for i in range(tensor_count)], axis=1)
    gate_out = jnp.dot(slot_rows, gate_full, preferred_element_type=jnp.float32)
    up_out = jnp.dot(slot_rows, up_full, preferred_element_type=jnp.float32)
    hidden = (jax.nn.silu(gate_out) * up_out).astype(jnp.bfloat16)
    hidden = lax.optimization_barrier(hidden)
    parts = 2 if slice_width % 256 == 0 else 1
    width = slice_width // parts
    down_parts = down_full.reshape(tensor_count, parts, width, down_full.shape[1])
    splits = [(mixing, lax.reduce_precision(mixing, 8, 7)) for mixing in mixers]
    pieces = []
    for part in range(parts):
        rounded = lax.dot_general(
            hidden,
            down_parts[:, part].reshape(tensor_count * width, down_full.shape[1]),
            (((1,), (1,)), ((), ())),
            preferred_element_type=jnp.float32,
        ).astype(jnp.bfloat16)
        summed = lax.psum_scatter(rounded, "tensor", scatter_dimension=1, tiled=True)
        returned = lax.all_to_all(
            summed.reshape(experts, count * capacity, width),
            "expert",
            split_axis=0,
            concat_axis=0,
            tiled=True,
        )
        mixtures = []
        for i, (mixing, high) in enumerate(splits):
            rows = returned[:, i * capacity : (i + 1) * capacity].reshape(slots, width)
            mixtures.append(
                sum(
                    (
                        lax.dot_general(
                            term.astype(jnp.bfloat16),
                            rows,
                            (((0,), (0,)), ((), ())),
                            preferred_element_type=jnp.float32,
                        )
                        for term in (high, mixing - high)
                    )
                )
            )
        if exchange:
            piece = lax.psum_scatter(
                jnp.concatenate(mixtures, axis=0).astype(jnp.bfloat16),
                "dp",
                scatter_dimension=0,
                tiled=True,
            ).astype(jnp.float32)
        else:
            piece = mixtures[0]
        pieces.append(piece)
    mixture = jnp.concatenate(pieces, axis=1)
    return (own_slice + mixture).astype(jnp.bfloat16)


def solution(mesh):
    in_specs = (
        P(("dp", "expert"), None),
        P(("dp", "expert"), "tensor"),
        P(("dp", "expert"), "tensor"),
        P(("dp", "expert"), "tensor"),
        P("tensor", None),
        P(),
        P(("dp", "expert"), None),
        P(("dp", "expert"), None),
        P("expert", "dp", "tensor"),
        P("expert", "dp", "tensor"),
        P("expert", "dp", "tensor"),
    )
    out_specs = P(("dp", "expert"), "tensor")
    return jax.shard_map(local, mesh=mesh, in_specs=in_specs, out_specs=out_specs, check_vma=False)
```

profile of v0, /device:TPU:0, one launch (start us, length us, event | category | flops | bytes accessed | tf_op | source)
XLA Modules:
  0.0 471.7 jit_solution(1408861958945248297)
XLA Ops:
  10.3 14.8 %all-gather = f32[1024,4]{0,1:T(4,128)S(1)} all-gather(f32[256,4]{0,1:T(4,128)S(1)} %pad_maximum_fusion.12), channel_id=2, replica_groups=mesh['dp'=4,'expert'=4,'tensor'=2] {'dp'}, dimensions={0}, use_global_device_ids=true | all-gather | bytes 20480 | tf_op jit(solution)/shard_map/all_gather | solution.py:85
  25.4 3.4 constant_dynamic-slice_fusion.2
  28.8 3.4 collective-permute-start.2
  34.1 3.3 collective-permute-start.5
  38.7 11.5 %collective-permute-done.2 = bf16[688,512]{1,0:T(8,128)(2,1)} collective-permute-done((bf16[688,512]{1,0:T(8,128)(2,1)}, bf16[688,512]{1,0:T(8,128)(2,1)}, u32[]{:S(2)}, u32[]{:S(2)}) %collective-permute-start.2) | collective-permute-done | bytes 704544 | tf_op jit(solution)/shard_map/ppermute | solution.py:73
  50.2 29.1 %collective-permute-start.3 = (bf16[688,512]{1,0:T(8,128)(2,1)S(1)}, bf16[688,512]{1,0:T(8,128)(2,1)}, u32[]{:S(2)}, u32[]{:S(2)}) collective-permute-start(bf16[688,512]{1,0:T(8,128)(2,1)S(1)} %get-tuple-element.62), channel_id=1, source_target_pairs={{0,8},{8,16},{16,24},{24,0},{1,9},{9,17},{17,25},{25,1},{2,10},{10... | collective-permute-start | bytes 2113544 | tf_op jit(solution)/shard_map/ppermute | solution.py:73
  79.2 45.1 %collective-permute-done.1 = bf16[688,512]{1,0:T(8,128)(2,1)} collective-permute-done((bf16[688,512]{1,0:T(8,128)(2,1)}, bf16[688,512]{1,0:T(8,128)(2,1)}, u32[]{:S(2)}, u32[]{:S(2)}) %collective-permute-start.1) | collective-permute-done | bytes 704544 | tf_op jit(solution)/shard_map/ppermute | solution.py:73
  128.0 2.7 fusion.100
  134.5 2.3 divide_convert_fusion
  136.8 2.3 convolution_convert_fusion.2
  139.5 11.1 %collective-permute-done.4 = bf16[688,512]{1,0:T(8,128)(2,1)} collective-permute-done((bf16[688,512]{1,0:T(8,128)(2,1)}, bf16[688,512]{1,0:T(8,128)(2,1)}, u32[]{:S(2)}, u32[]{:S(2)}) %collective-permute-start.4) | collective-permute-done | bytes 704544 | tf_op jit(solution)/shard_map/ppermute | solution.py:73
  154.3 2.8 all-reduce.2.cloned.1.call-done
  164.1 44.2 %all-gather.9.cloned.1.call-done = bf16[1024,1024]{1,0:T(8,128)(2,1)} async-done(((bf16[256,1024]{1,0:T(8,128)(2,1)}), bf16[1024,1024]{1,0:T(8,128)(2,1)}) %all-gather.9.cloned.1.call-update) | async-done | bytes 2097168 | tf_op jit(solution)/shard_map/all_gather | solution.py:107
  212.5 2.4 pad_maximum_fusion.3
  214.8 5.2 %all-to-all-start = ((bf16[4,576,1024]{2,1,0:T(8,128)(2,1)}), bf16[4,576,1024]{2,1,0:T(8,128)(2,1)}, u32[]{:S(2)}, u32[]{:S(2)}) async-start(bf16[4,576,1024]{2,1,0:T(8,128)(2,1)} %pad_maximum_fusion.3), calls=%async_computation | async-start | bytes 9437184 | tf_op jit(solution)/shard_map/all_to_all | solution.py:125
  223.5 15.5 %collective-permute-done.8 = bf16[688,512]{1,0:T(8,128)(2,1)S(1)} collective-permute-done((bf16[688,512]{1,0:T(8,128)(2,1)S(1)}, bf16[688,512]{1,0:T(8,128)(2,1)S(1)}, u32[]{:S(2)}, u32[]{:S(2)}) %collective-permute-start.8) | collective-permute-done | bytes 704544 | tf_op jit(solution)/shard_map/ppermute | solution.py:73
  238.9 43.6 %collective-permute-done.7 = bf16[688,512]{1,0:T(8,128)(2,1)S(1)} collective-permute-done((bf16[688,512]{1,0:T(8,128)(2,1)S(1)}, bf16[688,512]{1,0:T(8,128)(2,1)S(1)}, u32[]{:S(2)}, u32[]{:S(2)}) %collective-permute-start.7) | collective-permute-done | bytes 704544 | tf_op jit(solution)/shard_map/ppermute | solution.py:73
  285.5 6.5 %reshape.189 = bf16[2,2,512,688]{2,1,0,3:T(2,128)(2,1)S(1)} reshape(bf16[2048,688]{0,1:T(8,128)(2,1)} %maximum_bitcast_fusion.2) | data formatting | bytes 5636096 | tf_op jit(solution)/shard_map/reshape | solution.py:138
  292.1 19.3 %slice_reduce_fusion.1 = (bf16[2,512,688]{1,0,2:T(2,128)(2,1)S(1)}, bf16[2,512,688]{1,0,2:T(2,128)(2,1)}) fusion(bf16[2,2,512,688]{2,1,0,3:T(2,128)(2,1)S(1)} %reshape.189), kind=kLoop, calls=%fused_computation.18 | loop fusion | bytes 5636096 | tf_op jit(solution)/shard_map/slice | solution.py:144
  312.9 7.3 %fusion.99 = (bf16[2304,1024]{1,0:T(8,128)(2,1)S(1)}, bf16[2304,1024]{1,0:T(8,128)(2,1)}) fusion(bf16[4608,1024]{1,0:T(8,128)(2,1)} %all-gather.11.cloned.1.call-done), kind=kLoop, calls=%fused_computation.212 | loop fusion | bytes 18874368 | tf_op jit(solution)/shard_map/slice | solution.py:131
  320.2 11.6 %fusion.1 = f32[2304,688]{0,1:T(8,128)} fusion(bf16[2048,688]{0,1:T(8,128)(2,1)S(1)} %copy-done.12, bf16[2304,1024]{1,0:T(8,128)(2,1)} %get-tuple-element.44, bf16[2304,1024]{1,0:T(8,128)(2,1)S(1)} %get-tuple-element.43), kind=kOutput, calls=%fused_computation.5 | convolution fusion | flops 6511656960 | bytes 18595840 | tf_op jit(solution)/shard_map/dot_general | solution.py:133
  331.7 9.6 %multiply_convert_fusion = bf16[2304,688]{0,1:T(8,128)(2,1)S(1)} fusion(f32[2304,688]{0,1:T(8,128)} %fusion.1, bf16[2048,688]{0,1:T(8,128)(2,1)S(1)} %copy-done.11, bf16[2304,1024]{1,0:T(8,128)(2,1)S(1)} %copy-done.8, bf16[2304,1024]{1,0:T(8,128)(2,1)S(1)} %get-tuple-element.43), kind=kOutput, calls=%fused_computation.4 | convolution fusion | flops 6521167872 | bytes 21766144 | tf_op jit(solution)/shard_map/dot_general | solution.py:132
  343.0 5.5 %convolution_convert_fusion.1 = bf16[2304,1024]{1,0:T(8,128)(2,1)} fusion(bf16[2304,688]{0,1:T(8,128)(2,1)S(1)} %multiply_convert_fusion, bf16[1024,688]{0,1:T(8,128)(2,1)S(1)} %bitcast.174), kind=kOutput, calls=%fused_computation.10 | convolution fusion | flops 3248750592 | bytes 9297920 | tf_op jit(solution)/shard_map/dot_general | solution.py:142
  350.2 7.6 %convolution_convert_fusion = bf16[2304,1024]{1,0:T(8,128)(2,1)} fusion(bf16[2304,688]{0,1:T(8,128)(2,1)} %copy-done.20, bf16[1024,688]{0,1:T(8,128)(2,1)S(1)} %bitcast.175), kind=kOutput, calls=%fused_computation.9 | convolution fusion | flops 3248750592 | bytes 9297920 | tf_op jit(solution)/shard_map/dot_general | solution.py:142
  357.8 4.2 reduce-scatter.5.cloned.1.call-done
  362.0 3.9 all-to-all-start.1
  366.6 11.4 %reduce-scatter.9.cloned.1.call-done = bf16[2304,512]{1,0:T(8,128)(2,1)} async-done(((bf16[2304,1024]{1,0:T(8,128)(2,1)}), bf16[2304,512]{1,0:T(8,128)(2,1)}) %reduce-scatter.9.cloned.1.call-update) | async-done | bytes 2359312 | tf_op jit(solution)/shard_map/reduce_scatter | solution.py:148
  378.0 16.1 %all-to-all-done.1 = bf16[4,576,512]{2,1,0:T(8,128)(2,1)S(1)} async-done(((bf16[4,576,512]{2,1,0:T(8,128)(2,1)}), bf16[4,576,512]{2,1,0:T(8,128)(2,1)S(1)}, u32[]{:S(2)}, u32[]{:S(2)}) %all-to-all-start.1) | async-done | bytes 2359328 | tf_op jit(solution)/shard_map/all_to_all | solution.py:149
  395.5 3.6 all-to-all-start.2
  405.7 20.7 %all-to-all-done.2 = bf16[4,576,512]{2,1,0:T(8,128)(2,1)S(1)} async-done(((bf16[4,576,512]{2,1,0:T(8,128)(2,1)}), bf16[4,576,512]{2,1,0:T(8,128)(2,1)S(1)}, u32[]{:S(2)}, u32[]{:S(2)}) %all-to-all-start.2) | async-done | bytes 2359328 | tf_op jit(solution)/shard_map/all_to_all | solution.py:149
  431.1 3.4 reduce-scatter.7.cloned.1.call-done
  434.5 28.1 %reduce-scatter.11.cloned.1.call-done = bf16[256,512]{1,0:T(8,128)(2,1)} async-done(((bf16[1024,512]{1,0:T(8,128)(2,1)}), bf16[256,512]{1,0:T(8,128)(2,1)}) %reduce-scatter.11.cloned.1.call-update) | async-done | bytes 262160 | tf_op jit(solution)/shard_map/reduce_scatter | solution.py:173
  (144 shorter events, 56.0 us)
Async XLA Ops:
  6.5 124.2 %copy-start = (bf16[256,1024]{1,0:T(8,128)(2,1)S(1)}, bf16[256,1024]{1,0:T(8,128)(2,1)}, u32[]{:S(2)}) copy-start(bf16[256,1024]{1,0:T(8,128)(2,1)} %param.12) | copy-start | bytes 1572868
  6.5 121.5 %all-gather.7.cloned.1.call-start = ((), (), s32[]{:S(2)}) async-start(), calls=%async_computation.7 | async-start | bytes 5242880 | tf_op jit(solution)/shard_map/all_gather | solution.py:83
  10.2 146.9 %all-reduce.2.cloned.1.call-start = ((), (), s32[]{:S(2)}) async-start(), calls=%async_computation.8 | async-start | bytes 2097152 | tf_op jit(solution)/shard_map/psum | solution.py:93
  25.4 138.0 %copy-start.2 = (f32[1024,4]{1,0:T(8,128)}, f32[1024,4]{1,0:T(8,128)S(1)}, u32[]{:S(2)}) copy-start(f32[1024,4]{1,0:T(8,128)S(1)} %copy.23) | copy-start | bytes 49156
  25.4 7.3 %copy-start.9 = (bf16[1,512,2752]{1,2,0:T(8,128)(2,1)S(1)}, bf16[1,512,2752]{1,2,0:T(8,128)(2,1)}, u32[]{:S(2)}) copy-start(bf16[1,512,2752]{1,2,0:T(8,128)(2,1)} %param.20) | copy-start | bytes 8454148
  28.8 21.4 %collective-permute-start.2 = (bf16[688,512]{1,0:T(8,128)(2,1)}, bf16[688,512]{1,0:T(8,128)(2,1)}, u32[]{:S(2)}, u32[]{:S(2)}) collective-permute-start(bf16[688,512]{1,0:T(8,128)(2,1)} %get-tuple-element.68), channel_id=1, source_target_pairs={{0,24},{8,0},{16,8},{24,16},{1,25},{9,1},{17,9},{25,17},{2,26},{10... | collective-permute-start | bytes 2113544 | tf_op jit(solution)/shard_map/ppermute | solution.py:73
  32.2 92.2 %collective-permute-start.1 = (bf16[688,512]{1,0:T(8,128)(2,1)}, bf16[688,512]{1,0:T(8,128)(2,1)}, u32[]{:S(2)}, u32[]{:S(2)}) collective-permute-start(bf16[688,512]{1,0:T(8,128)(2,1)} %get-tuple-element.69), channel_id=1, source_target_pairs={{0,16},{8,24},{16,0},{24,8},{1,17},{9,25},{17,1},{25,9},{2,18},{10... | collective-permute-start | bytes 2113544 | tf_op jit(solution)/shard_map/ppermute | solution.py:73
  32.2 92.2 %collective-permute-start = (bf16[688,512]{1,0:T(8,128)(2,1)}, bf16[688,512]{1,0:T(8,128)(2,1)}, u32[]{:S(2)}, u32[]{:S(2)}) collective-permute-start(bf16[688,512]{1,0:T(8,128)(2,1)} %get-tuple-element.70), channel_id=1, source_target_pairs={{0,8},{8,16},{16,24},{24,0},{1,9},{9,17},{17,25},{25,1},{2,10},{10... | collective-permute-start | bytes 2113544 | tf_op jit(solution)/shard_map/ppermute | solution.py:73
  34.1 105.4 %collective-permute-start.5 = (bf16[688,512]{1,0:T(8,128)(2,1)}, bf16[688,512]{1,0:T(8,128)(2,1)}, u32[]{:S(2)}, u32[]{:S(2)}) collective-permute-start(bf16[688,512]{1,0:T(8,128)(2,1)} %get-tuple-element.60), channel_id=1, source_target_pairs={{0,24},{8,0},{16,8},{24,16},{1,25},{9,1},{17,9},{25,17},{2,26},{10... | collective-permute-start | bytes 2113544 | tf_op jit(solution)/shard_map/ppermute | solution.py:73
  37.4 113.2 %collective-permute-start.4 = (bf16[688,512]{1,0:T(8,128)(2,1)}, bf16[688,512]{1,0:T(8,128)(2,1)}, u32[]{:S(2)}, u32[]{:S(2)}) collective-permute-start(bf16[688,512]{1,0:T(8,128)(2,1)} %get-tuple-element.61), channel_id=1, source_target_pairs={{0,16},{8,24},{16,0},{24,8},{1,17},{9,25},{17,1},{25,9},{2,18},{10... | collective-permute-start | bytes 2113544 | tf_op jit(solution)/shard_map/ppermute | solution.py:73
  50.2 100.4 %collective-permute-start.3 = (bf16[688,512]{1,0:T(8,128)(2,1)S(1)}, bf16[688,512]{1,0:T(8,128)(2,1)}, u32[]{:S(2)}, u32[]{:S(2)}) collective-permute-start(bf16[688,512]{1,0:T(8,128)(2,1)S(1)} %get-tuple-element.62), channel_id=1, source_target_pairs={{0,8},{8,16},{16,24},{24,0},{1,9},{9,17},{17,25},{25,1},{2,10},{10... | collective-permute-start | bytes 2113544 | tf_op jit(solution)/shard_map/ppermute | solution.py:73
  139.1 69.2 %all-gather.9.cloned.1.call-start = ((), (), s32[]{:S(2)}) async-start(), calls=%async_computation.13 | async-start | bytes 2621440 | tf_op jit(solution)/shard_map/all_gather | solution.py:107
  152.5 4.6 copy-start.14
  214.8 5.2 %copy-start.10 = (bf16[1,512,2752]{1,2,0:T(8,128)(2,1)S(1)}, bf16[1,512,2752]{1,2,0:T(8,128)(2,1)}, u32[]{:S(2)}) copy-start(bf16[1,512,2752]{1,2,0:T(8,128)(2,1)} %param.21) | copy-start | bytes 8454148
  214.8 70.1 %all-to-all-start = ((bf16[4,576,1024]{2,1,0:T(8,128)(2,1)}), bf16[4,576,1024]{2,1,0:T(8,128)(2,1)}, u32[]{:S(2)}, u32[]{:S(2)}) async-start(bf16[4,576,1024]{2,1,0:T(8,128)(2,1)} %pad_maximum_fusion.3), calls=%async_computation | async-start | bytes 9437184 | tf_op jit(solution)/shard_map/all_to_all | solution.py:125
  220.0 92.9 %all-gather.11.cloned.1.call-start = ((), (), s32[]{:S(2)}) async-start(), calls=%async_computation.14 | async-start | bytes 14155776 | tf_op jit(solution)/shard_map/all_gather | solution.py:130
  220.3 18.6 %collective-permute-start.8 = (bf16[688,512]{1,0:T(8,128)(2,1)S(1)}, bf16[688,512]{1,0:T(8,128)(2,1)S(1)}, u32[]{:S(2)}, u32[]{:S(2)}) collective-permute-start(bf16[688,512]{1,0:T(8,128)(2,1)S(1)} %get-tuple-element.52), channel_id=1, source_target_pairs={{0,24},{8,0},{16,8},{24,16},{1,25},{9,1},{17,9},{25,17},{2,26},{10... | collective-permute-start | bytes 2113544 | tf_op jit(solution)/shard_map/ppermute | solution.py:73
  221.5 61.0 %collective-permute-start.7 = (bf16[688,512]{1,0:T(8,128)(2,1)S(1)}, bf16[688,512]{1,0:T(8,128)(2,1)S(1)}, u32[]{:S(2)}, u32[]{:S(2)}) collective-permute-start(bf16[688,512]{1,0:T(8,128)(2,1)S(1)} %get-tuple-element.53), channel_id=1, source_target_pairs={{0,16},{8,24},{16,0},{24,8},{1,17},{9,25},{17,1},{25,9},{2,18},{10... | collective-permute-start | bytes 2113544 | tf_op jit(solution)/shard_map/ppermute | solution.py:73
  221.7 60.8 %collective-permute-start.6 = (bf16[688,512]{1,0:T(8,128)(2,1)S(1)}, bf16[688,512]{1,0:T(8,128)(2,1)S(1)}, u32[]{:S(2)}, u32[]{:S(2)}) collective-permute-start(bf16[688,512]{1,0:T(8,128)(2,1)S(1)} %get-tuple-element.54), channel_id=1, source_target_pairs={{0,8},{8,16},{16,24},{24,0},{1,9},{9,17},{17,25},{25,1},{2,10},{10... | collective-permute-start | bytes 2113544 | tf_op jit(solution)/shard_map/ppermute | solution.py:73
  285.0 77.0 %reduce-scatter.5.cloned.1.call-start = ((), (), s32[]{:S(2)}) async-start(), calls=%async_computation.9 | async-start | bytes 7077888 | tf_op jit(solution)/shard_map/reduce_scatter | solution.py:148
  312.9 7.3 %copy-start.12 = (bf16[2048,688]{0,1:T(8,128)(2,1)S(1)}, bf16[2048,688]{0,1:T(8,128)(2,1)}, u32[]{:S(2)}) copy-start(bf16[2048,688]{0,1:T(8,128)(2,1)} %maximum_bitcast_fusion.1) | copy-start | bytes 8454148
  320.2 11.6 %copy-start.8 = (bf16[2304,1024]{1,0:T(8,128)(2,1)S(1)}, bf16[2304,1024]{1,0:T(8,128)(2,1)}, u32[]{:S(2)}) copy-start(bf16[2304,1024]{1,0:T(8,128)(2,1)} %get-tuple-element.44) | copy-start | bytes 14155780
  320.2 11.6 %copy-start.11 = (bf16[2048,688]{0,1:T(8,128)(2,1)S(1)}, bf16[2048,688]{0,1:T(8,128)(2,1)}, u32[]{:S(2)}) copy-start(bf16[2048,688]{0,1:T(8,128)(2,1)} %maximum_bitcast_fusion) | copy-start | bytes 8454148
  331.7 11.3 %copy-start.13 = (bf16[86,8,2,512]{3,1,2,0:T(8,128)(2,1)S(1)}, bf16[86,8,2,512]{3,1,2,0:T(8,128)(2,1)}, u32[]{:S(2)}) copy-start(bf16[86,8,2,512]{3,1,2,0:T(8,128)(2,1)} %copy.30) | copy-start | bytes 4227076
  348.5 29.4 %reduce-scatter.9.cloned.1.call-start = ((), (), s32[]{:S(2)}) async-start(), calls=%async_computation.11 | async-start | bytes 7077888 | tf_op jit(solution)/shard_map/reduce_scatter | solution.py:148
  357.8 8.1 %copy-start.3 = (f32[1024,4]{1,0:T(8,128)S(1)}, f32[1024,4]{1,0:T(8,128)}, u32[]{:S(2)}) copy-start(f32[1024,4]{1,0:T(8,128)} %copy-done.2) | copy-start | bytes 49156
  362.0 32.0 %all-to-all-start.1 = ((bf16[4,576,512]{2,1,0:T(8,128)(2,1)}), bf16[4,576,512]{2,1,0:T(8,128)(2,1)S(1)}, u32[]{:S(2)}, u32[]{:S(2)}) async-start(bf16[4,576,512]{2,1,0:T(8,128)(2,1)} %bitcast.172), calls=%async_computation.2 | async-start | bytes 4718592 | tf_op jit(solution)/shard_map/all_to_all | solution.py:149
  395.5 30.9 %all-to-all-start.2 = ((bf16[4,576,512]{2,1,0:T(8,128)(2,1)}), bf16[4,576,512]{2,1,0:T(8,128)(2,1)S(1)}, u32[]{:S(2)}, u32[]{:S(2)}) async-start(bf16[4,576,512]{2,1,0:T(8,128)(2,1)} %bitcast.171), calls=%async_computation.5 | async-start | bytes 4718592 | tf_op jit(solution)/shard_map/all_to_all | solution.py:149
  399.1 35.4 %reduce-scatter.7.cloned.1.call-start = ((), (), s32[]{:S(2)}) async-start(), calls=%async_computation.10 | async-start | bytes 1310720 | tf_op jit(solution)/shard_map/reduce_scatter | solution.py:173
  405.6 57.0 %reduce-scatter.11.cloned.1.call-start = ((), (), s32[]{:S(2)}) async-start(), calls=%async_computation.12 | async-start | bytes 1310720 | tf_op jit(solution)/shard_map/reduce_scatter | solution.py:173
  429.5 33.1 %copy-start.6 = (f32[256,2048]{1,0:T(8,128)S(1)}, f32[256,2048]{1,0:T(8,128)}, u32[]{:S(2)}) copy-start(f32[256,2048]{1,0:T(8,128)} %copy-done.5) | copy-start | bytes 6291460
  429.5 35.1 %copy-start.1 = (bf16[256,1024]{1,0:T(8,128)(2,1)S(1)}, bf16[256,1024]{1,0:T(8,128)(2,1)}, u32[]{:S(2)}) copy-start(bf16[256,1024]{1,0:T(8,128)(2,1)} %param.12) | copy-start | bytes 1572868
  (9 other events, 21.4 us)
Sparse Core Ops, SparseCore 0:
  10.3 55.2 all-gather.6
  139.2 17.7 all-reduce.1
  161.2 47.1 all-gather.8
  285.1 22.5 all-gather.10
  348.7 13.3 reduce-scatter.4
  364.2 13.7 reduce-scatter.8
  405.8 28.7 reduce-scatter.6
  436.8 25.7 reduce-scatter.10
where the time goes:
time: 479 us; the launch traced here: 472 us
  waiting for transfers between devices  258 us (54%)
  local copies, waits for them, and re-layouts  56.1 us (12%)
  starting transfers between devices  54.6 us (11%)
  matrix products  52.3 us (11%)
  other arithmetic  21.6 us (5%)
  blocking collectives  14.8 us (3%)
  between operations  14.4 us (3%)
    ppermute x9, waiting for transfers between devices, spread(): lax.ppermute(block, 'dp', [(i, (i + step) % copies) for i in range(copies)])  127 us
    all_gather x1, waiting for transfers between devices, local(): lax.all_gather(own_cols, 'dp', axis=0)  44.2 us
    ppermute x9, starting transfers between devices, spread(): lax.ppermute(block, 'dp', [(i, (i + step) % copies) for i in range(copies)])  40.5 us
    all_to_all x2, waiting for transfers between devices, local(): lax.all_to_all(summed.reshape(experts, count * capacity, width), 'expert'...  36.8 us
    reduce_scatter x2, waiting for transfers between devices, local(): lax.psum_scatter(jnp.concatenate(mixtures, axis=0).astype(jnp.bfloat16),...  31.6 us
    slice x1, local copies, waits for them, and re-layouts, local(): down_parts[:, part].reshape(tensor_count * width, down_full.shape[1])  19.3 us
    reduce_scatter x2, waiting for transfers between devices, local(): lax.psum_scatter(rounded, 'tensor', scatter_dimension=1, tiled=True)  15.6 us
    all_gather x1, blocking collectives, local(): choice = lax.all_gather(choice, 'dp', axis=0)  14.8 us
  transfers between devices with their start and end apart: 20, of which 13 were waited for; matrix products, arithmetic and copies ran while one was open for 16% of the time, Pallas kernels for 0%

commit v1 on v0

--- a/solution.py
+++ b/solution.py
@@ -6,6 +6,22 @@
 HDIM = 128
 EPSILON = 1e-05
 NEGATIVE = -1e30
+
+
+def swapped_with_each(x, axis, split, join):
+    ways, here = (lax.axis_size(axis), lax.axis_index(axis))
+    width = x.shape[split] // ways
+    shape = list(x.shape)
+    shape[split] = width
+    height = shape[join]
+    shape[join] = height * ways
+    full = jnp.zeros(shape, x.dtype)
+    for mask in range(ways):
+        part = lax.dynamic_slice_in_dim(x, (here ^ mask) * width, width, axis=split)
+        if mask:
+            part = lax.ppermute(part, axis, [(d, d ^ mask) for d in range(ways)])
+        full = lax.dynamic_update_slice_in_dim(full, part, (here ^ mask) * height, axis=join)
+    return full
 
 
 def slot_table(block_routes, experts, capacity):
@@ -146,12 +162,8 @@
             preferred_element_type=jnp.float32,
         ).astype(jnp.bfloat16)
         summed = lax.psum_scatter(rounded, "tensor", scatter_dimension=1, tiled=True)
-        returned = lax.all_to_all(
-            summed.reshape(experts, count * capacity, width),
-            "expert",
-            split_axis=0,
-            concat_axis=0,
-            tiled=True,
+        returned = swapped_with_each(
+            summed.reshape(experts, count * capacity, width), "expert", 0, 0
         )
         mixtures = []
         for i, (mixing, high) in enumerate(splits):

time: 479 us -> 478 us (level)
  waiting for transfers between devices: 258 us -> 244 us
  local copies, waits for them, and re-layouts: 56.1 us -> 68.6 us
    all_to_all x2 -> x0, waiting for transfers between devices: 36.8 us -> none  [local(): lax.all_to_all(summed.reshape(experts, count * capacity, width), 'expert'...]
    ppermute x0 -> x6, waiting for transfers between devices: none -> 22.8 us  [swapped_with_each(): part = lax.ppermute(part, axis, [(d, d ^ mask) for d in range(ways)])]
    dynamic_update_slice x0 -> x6, local copies, waits for them, and re-layouts: none -> 8.04 us  [swapped_with_each(): lax.dynamic_update_slice_in_dim(full, part, (here ^ mask) * height, axis=...]
    ppermute x0 -> x6, starting transfers between devices: none -> 7.62 us  [swapped_with_each(): part = lax.ppermute(part, axis, [(d, d ^ mask) for d in range(ways)])]
    all_to_all x2 -> x0, starting transfers between devices: 7.52 us -> none  [local(): lax.all_to_all(summed.reshape(experts, count * capacity, width), 'expert'...]
    unnamed x46 -> x48, local copies, waits for them, and re-layouts: 10.1 us -> 11 us
  transfers between devices with their start and end apart: 20 -> 24, of which waited for: 13 -> 14; matrix products, arithmetic and copies ran while one was open for 16% -> 19% of each run, Pallas kernels for 0% -> 0%
where the time goes in v1:
time: 478 us; the launch traced here: 470 us
  waiting for transfers between devices  244 us (51%)
  local copies, waits for them, and re-layouts  68.6 us (14%)
  starting transfers between devices  54.7 us (11%)
  matrix products  52.3 us (11%)
  other arithmetic  21.6 us (5%)
  blocking collectives  14.8 us (3%)
  between operations  14.5 us (3%)
    ppermute x9, waiting for transfers between devices, spread(): lax.ppermute(block, 'dp', [(i, (i + step) % copies) for i in range(copies)])  127 us
    all_gather x1, waiting for transfers between devices, local(): lax.all_gather(own_cols, 'dp', axis=0)  44.2 us
    ppermute x9, starting transfers between devices, spread(): lax.ppermute(block, 'dp', [(i, (i + step) % copies) for i in range(copies)])  40.5 us
    reduce_scatter x2, waiting for transfers between devices, local(): lax.psum_scatter(jnp.concatenate(mixtures, axis=0).astype(jnp.bfloat16),...  35.4 us
    ppermute x6, waiting for transfers between devices, swapped_with_each(): part = lax.ppermute(part, axis, [(d, d ^ mask) for d in range(ways)])  22.8 us
    slice x1, local copies, waits for them, and re-layouts, local(): down_parts[:, part].reshape(tensor_count * width, down_full.shape[1])  18.4 us
    all_gather x1, blocking collectives, local(): choice = lax.all_gather(choice, 'dp', axis=0)  14.8 us
    dot_general x2, matrix products, local(): lax.dot_general(hidden, down_parts[:, part].reshape(tensor_count * width,...  13.1 us
  transfers between devices with their start and end apart: 24, of which 14 were waited for; matrix products, arithmetic and copies ran while one was open for 19% of the time, Pallas kernels for 0%

profile of v1, /device:TPU:0, one launch (start us, length us, event | category | flops | bytes accessed | tf_op | source)
XLA Modules:
  0.0 470.5 jit_solution(7843093717492286274)
XLA Ops:
  10.3 14.8 %all-gather = f32[1024,4]{0,1:T(4,128)S(1)} all-gather(f32[256,4]{0,1:T(4,128)S(1)} %pad_maximum_fusion.12), channel_id=2, replica_groups=mesh['dp'=4,'expert'=4,'tensor'=2] {'dp'}, dimensions={0}, use_global_device_ids=true | all-gather | bytes 20480 | tf_op jit(solution)/shard_map/all_gather | solution.py:101
  25.4 3.4 constant_dynamic-slice_fusion.8
  28.8 3.4 collective-permute-start.2
  34.1 3.3 collective-permute-start.5
  38.7 11.5 %collective-permute-done.2 = bf16[688,512]{1,0:T(8,128)(2,1)} collective-permute-done((bf16[688,512]{1,0:T(8,128)(2,1)}, bf16[688,512]{1,0:T(8,128)(2,1)}, u32[]{:S(2)}, u32[]{:S(2)}) %collective-permute-start.2) | collective-permute-done | bytes 704544 | tf_op jit(solution)/shard_map/ppermute | solution.py:89
  50.2 29.1 %collective-permute-start.3 = (bf16[688,512]{1,0:T(8,128)(2,1)S(1)}, bf16[688,512]{1,0:T(8,128)(2,1)}, u32[]{:S(2)}, u32[]{:S(2)}) collective-permute-start(bf16[688,512]{1,0:T(8,128)(2,1)S(1)} %get-tuple-element.62), channel_id=1, source_target_pairs={{0,8},{8,16},{16,24},{24,0},{1,9},{9,17},{17,25},{25,1},{2,10},{10... | collective-permute-start | bytes 2113544 | tf_op jit(solution)/shard_map/ppermute | solution.py:89
  79.2 45.1 %collective-permute-done.1 = bf16[688,512]{1,0:T(8,128)(2,1)} collective-permute-done((bf16[688,512]{1,0:T(8,128)(2,1)}, bf16[688,512]{1,0:T(8,128)(2,1)}, u32[]{:S(2)}, u32[]{:S(2)}) %collective-permute-start.1) | collective-permute-done | bytes 704544 | tf_op jit(solution)/shard_map/ppermute | solution.py:89
  128.0 2.7 fusion.100
  132.4 2.0 fusion.3
  134.5 2.3 divide_convert_fusion
  136.8 2.3 convolution_convert_fusion.2
  139.5 11.1 %collective-permute-done.4 = bf16[688,512]{1,0:T(8,128)(2,1)} collective-permute-done((bf16[688,512]{1,0:T(8,128)(2,1)}, bf16[688,512]{1,0:T(8,128)(2,1)}, u32[]{:S(2)}, u32[]{:S(2)}) %collective-permute-start.4) | collective-permute-done | bytes 704544 | tf_op jit(solution)/shard_map/ppermute | solution.py:89
  154.3 2.8 all-reduce.2.cloned.1.call-done
  164.1 44.2 %all-gather.9.cloned.1.call-done = bf16[1024,1024]{1,0:T(8,128)(2,1)} async-done(((bf16[256,1024]{1,0:T(8,128)(2,1)}), bf16[1024,1024]{1,0:T(8,128)(2,1)}) %all-gather.9.cloned.1.call-update) | async-done | bytes 2097168 | tf_op jit(solution)/shard_map/all_gather | solution.py:123
  212.5 2.4 pad_maximum_fusion.3
  214.8 5.2 %all-to-all-start = ((bf16[4,576,1024]{2,1,0:T(8,128)(2,1)}), bf16[4,576,1024]{2,1,0:T(8,128)(2,1)}, u32[]{:S(2)}, u32[]{:S(2)}) async-start(bf16[4,576,1024]{2,1,0:T(8,128)(2,1)} %pad_maximum_fusion.3), calls=%async_computation | async-start | bytes 9437184 | tf_op jit(solution)/shard_map/all_to_all | solution.py:141
  223.5 15.5 %collective-permute-done.8 = bf16[688,512]{1,0:T(8,128)(2,1)S(1)} collective-permute-done((bf16[688,512]{1,0:T(8,128)(2,1)S(1)}, bf16[688,512]{1,0:T(8,128)(2,1)S(1)}, u32[]{:S(2)}, u32[]{:S(2)}) %collective-permute-start.8) | collective-permute-done | bytes 704544 | tf_op jit(solution)/shard_map/ppermute | solution.py:89
  238.9 43.6 %collective-permute-done.7 = bf16[688,512]{1,0:T(8,128)(2,1)S(1)} collective-permute-done((bf16[688,512]{1,0:T(8,128)(2,1)S(1)}, bf16[688,512]{1,0:T(8,128)(2,1)S(1)}, u32[]{:S(2)}, u32[]{:S(2)}) %collective-permute-start.7) | collective-permute-done | bytes 704544 | tf_op jit(solution)/shard_map/ppermute | solution.py:89
  285.5 6.5 %reshape.189 = bf16[2,2,512,688]{2,1,0,3:T(2,128)(2,1)S(1)} reshape(bf16[2048,688]{0,1:T(8,128)(2,1)} %maximum_bitcast_fusion.2) | data formatting | bytes 5636096 | tf_op jit(solution)/shard_map/reshape | solution.py:154
  292.0 18.4 %slice_reduce_fusion.1 = (bf16[2,512,688]{1,0,2:T(2,128)(2,1)}, bf16[2,512,688]{1,0,2:T(2,128)(2,1)S(1)}) fusion(bf16[2,2,512,688]{2,1,0,3:T(2,128)(2,1)S(1)} %reshape.189), kind=kLoop, calls=%fused_computation.18 | loop fusion | bytes 5636096 | tf_op jit(solution)/shard_map/slice | solution.py:160
  311.9 7.3 %fusion.99 = (bf16[2304,1024]{1,0:T(8,128)(2,1)S(1)}, bf16[2304,1024]{1,0:T(8,128)(2,1)}) fusion(bf16[4608,1024]{1,0:T(8,128)(2,1)} %all-gather.11.cloned.1.call-done), kind=kLoop, calls=%fused_computation.226 | loop fusion | bytes 18874368 | tf_op jit(solution)/shard_map/slice | solution.py:147
  319.2 11.6 %fusion.1 = f32[2304,688]{0,1:T(8,128)} fusion(bf16[2048,688]{0,1:T(8,128)(2,1)S(1)} %copy-done.11, bf16[2304,1024]{1,0:T(8,128)(2,1)} %get-tuple-element.44, bf16[2304,1024]{1,0:T(8,128)(2,1)S(1)} %get-tuple-element.43), kind=kOutput, calls=%fused_computation.5 | convolution fusion | flops 6511656960 | bytes 18595840 | tf_op jit(solution)/shard_map/dot_general | solution.py:149
  330.8 9.6 %multiply_convert_fusion = bf16[2304,688]{0,1:T(8,128)(2,1)S(1)} fusion(f32[2304,688]{0,1:T(8,128)} %fusion.1, bf16[2048,688]{0,1:T(8,128)(2,1)S(1)} %copy-done.10, bf16[2304,1024]{1,0:T(8,128)(2,1)S(1)} %copy-done.7, bf16[2304,1024]{1,0:T(8,128)(2,1)S(1)} %get-tuple-element.43), kind=kOutput, calls=%fused_computation.4 | convolution fusion | flops 6521167872 | bytes 21766144 | tf_op jit(solution)/shard_map/dot_general | solution.py:148
  342.0 5.6 %convolution_convert_fusion = bf16[2304,1024]{1,0:T(8,128)(2,1)} fusion(bf16[2304,688]{0,1:T(8,128)(2,1)S(1)} %multiply_convert_fusion, bf16[1024,688]{0,1:T(8,128)(2,1)S(1)} %bitcast.174), kind=kOutput, calls=%fused_computation.9 | convolution fusion | flops 3248750592 | bytes 9297920 | tf_op jit(solution)/shard_map/dot_general | solution.py:158
  349.3 7.5 %convolution_convert_fusion.1 = bf16[2304,1024]{1,0:T(8,128)(2,1)} fusion(bf16[2304,688]{0,1:T(8,128)(2,1)} %copy-done.21, bf16[1024,688]{0,1:T(8,128)(2,1)S(1)} %bitcast.175), kind=kOutput, calls=%fused_computation.10 | convolution fusion | flops 3248750592 | bytes 9297920 | tf_op jit(solution)/shard_map/dot_general | solution.py:158
  357.1 4.0 reduce-scatter.9.cloned.1.call-done
  369.2 7.9 %reduce-scatter.5.cloned.1.call-done = bf16[2304,512]{1,0:T(8,128)(2,1)} async-done(((bf16[2304,1024]{1,0:T(8,128)(2,1)}), bf16[2304,512]{1,0:T(8,128)(2,1)}) %reduce-scatter.5.cloned.1.call-update) | async-done | bytes 2359312 | tf_op jit(solution)/shard_map/reduce_scatter | solution.py:164
  386.1 8.8 %collective-permute-done.13 = bf16[1,576,512]{2,1,0:T(8,128)(2,1)} collective-permute-done((bf16[1,576,512]{2,1,0:T(8,128)(2,1)}, bf16[1,576,512]{2,1,0:T(8,128)(2,1)}, u32[]{:S(2)}, u32[]{:S(2)}) %collective-permute-start.13) | collective-permute-done | bytes 589856 | tf_op jit(solution)/shard_map/ppermute | solution.py:22
  408.0 12.2 %collective-permute-done.10 = bf16[1,576,512]{2,1,0:T(8,128)(2,1)S(1)} collective-permute-done((bf16[1,576,512]{2,1,0:T(8,128)(2,1)}, bf16[1,576,512]{2,1,0:T(8,128)(2,1)S(1)}, u32[]{:S(2)}, u32[]{:S(2)}) %collective-permute-start.10) | collective-permute-done | bytes 589856 | tf_op jit(solution)/shard_map/ppermute | solution.py:22
  426.0 7.3 %reduce-scatter.11.cloned.1.call-done = bf16[256,512]{1,0:T(8,128)(2,1)} async-done(((bf16[1024,512]{1,0:T(8,128)(2,1)}), bf16[256,512]{1,0:T(8,128)(2,1)}) %reduce-scatter.11.cloned.1.call-update) | async-done | bytes 262160 | tf_op jit(solution)/shard_map/reduce_scatter | solution.py:185
  433.3 28.1 %reduce-scatter.7.cloned.1.call-done = bf16[256,512]{1,0:T(8,128)(2,1)} async-done(((bf16[1024,512]{1,0:T(8,128)(2,1)}), bf16[256,512]{1,0:T(8,128)(2,1)}) %reduce-scatter.7.cloned.1.call-update) | async-done | bytes 262160 | tf_op jit(solution)/shard_map/reduce_scatter | solution.py:185
  461.5 2.0 add_convert_fusion
  (164 shorter events, 74.9 us)
Async XLA Ops:
  6.5 124.2 %copy-start = (bf16[256,1024]{1,0:T(8,128)(2,1)S(1)}, bf16[256,1024]{1,0:T(8,128)(2,1)}, u32[]{:S(2)}) copy-start(bf16[256,1024]{1,0:T(8,128)(2,1)} %param.12) | copy-start | bytes 1572868
  6.5 121.5 %all-gather.7.cloned.1.call-start = ((), (), s32[]{:S(2)}) async-start(), calls=%async_computation.5 | async-start | bytes 5242880 | tf_op jit(solution)/shard_map/all_gather | solution.py:99
  10.2 146.9 %all-reduce.2.cloned.1.call-start = ((), (), s32[]{:S(2)}) async-start(), calls=%async_computation.6 | async-start | bytes 2097152 | tf_op jit(solution)/shard_map/psum | solution.py:109
  25.3 138.0 %copy-start.2 = (f32[1024,4]{1,0:T(8,128)}, f32[1024,4]{1,0:T(8,128)S(1)}, u32[]{:S(2)}) copy-start(f32[1024,4]{1,0:T(8,128)S(1)} %copy.23) | copy-start | bytes 49156
  25.4 7.3 %copy-start.8 = (bf16[1,512,2752]{1,2,0:T(8,128)(2,1)S(1)}, bf16[1,512,2752]{1,2,0:T(8,128)(2,1)}, u32[]{:S(2)}) copy-start(bf16[1,512,2752]{1,2,0:T(8,128)(2,1)} %param.20) | copy-start | bytes 8454148
  28.8 21.4 %collective-permute-start.2 = (bf16[688,512]{1,0:T(8,128)(2,1)}, bf16[688,512]{1,0:T(8,128)(2,1)}, u32[]{:S(2)}, u32[]{:S(2)}) collective-permute-start(bf16[688,512]{1,0:T(8,128)(2,1)} %get-tuple-element.68), channel_id=1, source_target_pairs={{0,24},{8,0},{16,8},{24,16},{1,25},{9,1},{17,9},{25,17},{2,26},{10... | collective-permute-start | bytes 2113544 | tf_op jit(solution)/shard_map/ppermute | solution.py:89
  32.2 92.2 %collective-permute-start.1 = (bf16[688,512]{1,0:T(8,128)(2,1)}, bf16[688,512]{1,0:T(8,128)(2,1)}, u32[]{:S(2)}, u32[]{:S(2)}) collective-permute-start(bf16[688,512]{1,0:T(8,128)(2,1)} %get-tuple-element.69), channel_id=1, source_target_pairs={{0,16},{8,24},{16,0},{24,8},{1,17},{9,25},{17,1},{25,9},{2,18},{10... | collective-permute-start | bytes 2113544 | tf_op jit(solution)/shard_map/ppermute | solution.py:89
  32.2 92.2 %collective-permute-start = (bf16[688,512]{1,0:T(8,128)(2,1)}, bf16[688,512]{1,0:T(8,128)(2,1)}, u32[]{:S(2)}, u32[]{:S(2)}) collective-permute-start(bf16[688,512]{1,0:T(8,128)(2,1)} %get-tuple-element.70), channel_id=1, source_target_pairs={{0,8},{8,16},{16,24},{24,0},{1,9},{9,17},{17,25},{25,1},{2,10},{10... | collective-permute-start | bytes 2113544 | tf_op jit(solution)/shard_map/ppermute | solution.py:89
  34.1 105.4 %collective-permute-start.5 = (bf16[688,512]{1,0:T(8,128)(2,1)}, bf16[688,512]{1,0:T(8,128)(2,1)}, u32[]{:S(2)}, u32[]{:S(2)}) collective-permute-start(bf16[688,512]{1,0:T(8,128)(2,1)} %get-tuple-element.60), channel_id=1, source_target_pairs={{0,24},{8,0},{16,8},{24,16},{1,25},{9,1},{17,9},{25,17},{2,26},{10... | collective-permute-start | bytes 2113544 | tf_op jit(solution)/shard_map/ppermute | solution.py:89
  37.4 113.2 %collective-permute-start.4 = (bf16[688,512]{1,0:T(8,128)(2,1)}, bf16[688,512]{1,0:T(8,128)(2,1)}, u32[]{:S(2)}, u32[]{:S(2)}) collective-permute-start(bf16[688,512]{1,0:T(8,128)(2,1)} %get-tuple-element.61), channel_id=1, source_target_pairs={{0,16},{8,24},{16,0},{24,8},{1,17},{9,25},{17,1},{25,9},{2,18},{10... | collective-permute-start | bytes 2113544 | tf_op jit(solution)/shard_map/ppermute | solution.py:89
  50.2 100.4 %collective-permute-start.3 = (bf16[688,512]{1,0:T(8,128)(2,1)S(1)}, bf16[688,512]{1,0:T(8,128)(2,1)}, u32[]{:S(2)}, u32[]{:S(2)}) collective-permute-start(bf16[688,512]{1,0:T(8,128)(2,1)S(1)} %get-tuple-element.62), channel_id=1, source_target_pairs={{0,8},{8,16},{16,24},{24,0},{1,9},{9,17},{17,25},{25,1},{2,10},{10... | collective-permute-start | bytes 2113544 | tf_op jit(solution)/shard_map/ppermute | solution.py:89
  139.1 69.2 %all-gather.9.cloned.1.call-start = ((), (), s32[]{:S(2)}) async-start(), calls=%async_computation.11 | async-start | bytes 2621440 | tf_op jit(solution)/shard_map/all_gather | solution.py:123
  214.8 70.1 %all-to-all-start = ((bf16[4,576,1024]{2,1,0:T(8,128)(2,1)}), bf16[4,576,1024]{2,1,0:T(8,128)(2,1)}, u32[]{:S(2)}, u32[]{:S(2)}) async-start(bf16[4,576,1024]{2,1,0:T(8,128)(2,1)} %pad_maximum_fusion.3), calls=%async_computation | async-start | bytes 9437184 | tf_op jit(solution)/shard_map/all_to_all | solution.py:141
  220.0 91.9 %all-gather.11.cloned.1.call-start = ((), (), s32[]{:S(2)}) async-start(), calls=%async_computation.12 | async-start | bytes 14155776 | tf_op jit(solution)/shard_map/all_gather | solution.py:146
  220.3 18.6 %collective-permute-start.8 = (bf16[688,512]{1,0:T(8,128)(2,1)S(1)}, bf16[688,512]{1,0:T(8,128)(2,1)S(1)}, u32[]{:S(2)}, u32[]{:S(2)}) collective-permute-start(bf16[688,512]{1,0:T(8,128)(2,1)S(1)} %get-tuple-element.52), channel_id=1, source_target_pairs={{0,24},{8,0},{16,8},{24,16},{1,25},{9,1},{17,9},{25,17},{2,26},{10... | collective-permute-start | bytes 2113544 | tf_op jit(solution)/shard_map/ppermute | solution.py:89
  221.5 61.0 %collective-permute-start.7 = (bf16[688,512]{1,0:T(8,128)(2,1)S(1)}, bf16[688,512]{1,0:T(8,128)(2,1)S(1)}, u32[]{:S(2)}, u32[]{:S(2)}) collective-permute-start(bf16[688,512]{1,0:T(8,128)(2,1)S(1)} %get-tuple-element.53), channel_id=1, source_target_pairs={{0,16},{8,24},{16,0},{24,8},{1,17},{9,25},{17,1},{25,9},{2,18},{10... | collective-permute-start | bytes 2113544 | tf_op jit(solution)/shard_map/ppermute | solution.py:89
  221.7 60.8 %collective-permute-start.6 = (bf16[688,512]{1,0:T(8,128)(2,1)S(1)}, bf16[688,512]{1,0:T(8,128)(2,1)S(1)}, u32[]{:S(2)}, u32[]{:S(2)}) collective-permute-start(bf16[688,512]{1,0:T(8,128)(2,1)S(1)} %get-tuple-element.54), channel_id=1, source_target_pairs={{0,8},{8,16},{16,24},{24,0},{1,9},{9,17},{17,25},{25,1},{2,10},{10... | collective-permute-start | bytes 2113544 | tf_op jit(solution)/shard_map/ppermute | solution.py:89
  285.0 76.2 %reduce-scatter.9.cloned.1.call-start = ((), (), s32[]{:S(2)}) async-start(), calls=%async_computation.9 | async-start | bytes 7077888 | tf_op jit(solution)/shard_map/reduce_scatter | solution.py:164
  319.2 11.6 %copy-start.7 = (bf16[2304,1024]{1,0:T(8,128)(2,1)S(1)}, bf16[2304,1024]{1,0:T(8,128)(2,1)}, u32[]{:S(2)}) copy-start(bf16[2304,1024]{1,0:T(8,128)(2,1)} %get-tuple-element.44) | copy-start | bytes 14155780
  319.2 11.6 %copy-start.10 = (bf16[2048,688]{0,1:T(8,128)(2,1)S(1)}, bf16[2048,688]{0,1:T(8,128)(2,1)}, u32[]{:S(2)}) copy-start(bf16[2048,688]{0,1:T(8,128)(2,1)} %maximum_bitcast_fusion) | copy-start | bytes 8454148
  330.8 11.3 %copy-start.14 = (bf16[86,8,2,512]{3,1,2,0:T(8,128)(2,1)S(1)}, bf16[86,8,2,512]{3,1,2,0:T(8,128)(2,1)}, u32[]{:S(2)}) copy-start(bf16[86,8,2,512]{3,1,2,0:T(8,128)(2,1)} %copy.31) | copy-start | bytes 4227076
  347.6 29.4 %reduce-scatter.5.cloned.1.call-start = ((), (), s32[]{:S(2)}) async-start(), calls=%async_computation.7 | async-start | bytes 7077888 | tf_op jit(solution)/shard_map/reduce_scatter | solution.py:164
  356.9 76.5 %reduce-scatter.11.cloned.1.call-start = ((), (), s32[]{:S(2)}) async-start(), calls=%async_computation.10 | async-start | bytes 1310720 | tf_op jit(solution)/shard_map/reduce_scatter | solution.py:185
  365.1 18.1 %collective-permute-start.12 = (bf16[1,576,512]{2,1,0:T(8,128)(2,1)}, bf16[1,576,512]{2,1,0:T(8,128)(2,1)}, u32[]{:S(2)}, u32[]{:S(2)}) collective-permute-start(bf16[1,576,512]{2,1,0:T(8,128)(2,1)} %get-tuple-element.85), channel_id=1, source_target_pairs={{0,2},{2,0},{4,6},{6,4},{1,3},{3,1},{5,7},{7,5},{8,10},{10,8},{12,... | collective-permute-start | bytes 1769480 | tf_op jit(solution)/shard_map/ppermute | solution.py:22
  366.8 28.2 %collective-permute-start.13 = (bf16[1,576,512]{2,1,0:T(8,128)(2,1)}, bf16[1,576,512]{2,1,0:T(8,128)(2,1)}, u32[]{:S(2)}, u32[]{:S(2)}) collective-permute-start(bf16[1,576,512]{2,1,0:T(8,128)(2,1)} %get-tuple-element.84), channel_id=1, source_target_pairs={{0,4},{2,6},{4,0},{6,2},{1,5},{3,7},{5,1},{7,3},{8,12},{10,14},{12... | collective-permute-start | bytes 1769480 | tf_op jit(solution)/shard_map/ppermute | solution.py:22
  368.3 28.6 %collective-permute-start.14 = (bf16[1,576,512]{2,1,0:T(8,128)(2,1)}, bf16[1,576,512]{2,1,0:T(8,128)(2,1)}, u32[]{:S(2)}, u32[]{:S(2)}) collective-permute-start(bf16[1,576,512]{2,1,0:T(8,128)(2,1)} %get-tuple-element.83), channel_id=1, source_target_pairs={{0,6},{2,4},{4,2},{6,0},{1,7},{3,5},{5,3},{7,1},{8,14},{10,12},{12... | collective-permute-start | bytes 1769480 | tf_op jit(solution)/shard_map/ppermute | solution.py:22
  380.0 26.8 %collective-permute-start.9 = (bf16[1,576,512]{2,1,0:T(8,128)(2,1)}, bf16[1,576,512]{2,1,0:T(8,128)(2,1)}, u32[]{:S(2)}, u32[]{:S(2)}) collective-permute-start(bf16[1,576,512]{2,1,0:T(8,128)(2,1)} %get-tuple-element.77), channel_id=1, source_target_pairs={{0,2},{2,0},{4,6},{6,4},{1,3},{3,1},{5,7},{7,5},{8,10},{10,8},{12,... | collective-permute-start | bytes 1769480 | tf_op jit(solution)/shard_map/ppermute | solution.py:22
  381.7 38.4 %collective-permute-start.10 = (bf16[1,576,512]{2,1,0:T(8,128)(2,1)}, bf16[1,576,512]{2,1,0:T(8,128)(2,1)S(1)}, u32[]{:S(2)}, u32[]{:S(2)}) collective-permute-start(bf16[1,576,512]{2,1,0:T(8,128)(2,1)} %get-tuple-element.76), channel_id=1, source_target_pairs={{0,4},{2,6},{4,0},{6,2},{1,5},{3,7},{5,1},{7,3},{8,12},{10,14},{12... | collective-permute-start | bytes 1769480 | tf_op jit(solution)/shard_map/ppermute | solution.py:22
  383.2 37.0 %collective-permute-start.11 = (bf16[1,576,512]{2,1,0:T(8,128)(2,1)}, bf16[1,576,512]{2,1,0:T(8,128)(2,1)}, u32[]{:S(2)}, u32[]{:S(2)}) collective-permute-start(bf16[1,576,512]{2,1,0:T(8,128)(2,1)} %get-tuple-element.75), channel_id=1, source_target_pairs={{0,6},{2,4},{4,2},{6,0},{1,7},{3,5},{5,3},{7,1},{8,14},{10,12},{12... | collective-permute-start | bytes 1769480 | tf_op jit(solution)/shard_map/ppermute | solution.py:22
  405.0 56.5 %reduce-scatter.7.cloned.1.call-start = ((), (), s32[]{:S(2)}) async-start(), calls=%async_computation.8 | async-start | bytes 1310720 | tf_op jit(solution)/shard_map/reduce_scatter | solution.py:185
  424.5 37.0 %copy-start.5 = (f32[256,2048]{1,0:T(8,128)S(1)}, f32[256,2048]{1,0:T(8,128)}, u32[]{:S(2)}) copy-start(f32[256,2048]{1,0:T(8,128)} %copy-done.4) | copy-start | bytes 6291460
  424.5 38.9 %copy-start.1 = (bf16[256,1024]{1,0:T(8,128)(2,1)S(1)}, bf16[256,1024]{1,0:T(8,128)(2,1)}, u32[]{:S(2)}) copy-start(bf16[256,1024]{1,0:T(8,128)(2,1)} %param.12) | copy-start | bytes 1572868
  (14 other events, 46.2 us)
Sparse Core Ops, SparseCore 0:
  10.3 55.2 all-gather.6
  139.2 17.8 all-reduce.1
  161.1 47.1 all-gather.8
  285.1 22.5 all-gather.10
  347.8 13.3 reduce-scatter.8
  363.3 13.7 reduce-scatter.4
  405.1 28.1 reduce-scatter.10
  435.6 25.7 reduce-scatter.6
